TPU v7x, 32 devices: a whole 2x2x4 slice. The times are simulated.
32 devices in a mesh: seq: 4 (over z), fsdp: 2 (over y), dp: 4 (over x, core).
Axes of the slice: x: 2, y: 2, z: 4, core: 2. Of those that a mesh axis runs over, the one named last changes fastest.
Arguments:
- query: bfloat16 [8, 768, 1024], P(('fsdp', 'dp'), 'seq'), may hold values from -6 to 6
- key: bfloat16 [8, 768, 1024], P(('fsdp', 'dp'), 'seq'), may hold values from -6 to 6
- value: bfloat16 [8, 768, 1024], P(('fsdp', 'dp'), 'seq'), may hold values from -4 to 4
- out_weight: bfloat16 [1024, 2048], P('fsdp'), may hold values from -0.1875 to 0.1875
- out_grad: bfloat16 [8, 768, 2048], P(('fsdp', 'dp'), 'seq'), may hold values from -5 to 5
- block_ids: int32 [8], P('seq'), may hold values from 0 to 7, as said below
Outputs:
- query_grad: bfloat16 [8, 768, 1024], P(('fsdp', 'dp'), 'seq')
- key_grad: bfloat16 [8, 768, 1024], P(('fsdp', 'dp'), 'seq')
- value_grad: bfloat16 [8, 768, 1024], P(('fsdp', 'dp'), 'seq')
- weight_grad: bfloat16 [1024, 2048], P('fsdp')
Inputs may be any that keep to these rules, and one draw needn't show every extreme that they name: `block_ids`: each number 0 to 7 appears once, and entries 2 i and 2 i + 1 always sum to 7.
All inputs are finite; a program needn't handle non-finite values.
Results may differ from a plain program's by a relative error of at most 0.027.
Values may be sent and summed in bfloat16 or wider, within the bound.
A program may use at most 64 MiB of HBM per device.

v0:
```python
import math

import jax
import jax.numpy as jnp
from jax import lax
from jax.sharding import PartitionSpec as P

HEADS = 8
HD = 128


def positions_of(block_list, block_rows):
    offsets = jnp.arange(block_rows, dtype=jnp.int32)
    return (block_list[:, None] * block_rows + offsets[None, :]).reshape(-1)


def shards(query, key, value, out_weight, out_grad, block_ids):
    tokens_here = query.shape[1]
    width_heads = query.shape[2]
    block_rows = tokens_here // block_ids.shape[0]
    score_scale = 1.0 / math.sqrt(HD)
    all_blocks = lax.all_gather(block_ids, "seq", axis=0, tiled=True)
    query_pos = positions_of(block_ids, block_rows)
    every_pos = positions_of(all_blocks, block_rows)
    key_all, value_all = (
        lax.all_gather(key, "seq", axis=1, tiled=True),
        lax.all_gather(value, "seq", axis=1, tiled=True),
    )
    query_heads = query[0].reshape(tokens_here, HEADS, HD)
    key_heads = key_all[0].reshape(-1, HEADS, HD)
    value_heads = value_all[0].reshape(-1, HEADS, HD)
    scores = (
        jnp.einsum("thd,khd->htk", query_heads, key_heads, preferred_element_type=jnp.float32)
        * score_scale
    )
    allowed = every_pos[None, :] <= query_pos[:, None]
    scores = jnp.where(allowed[None], scores, -jnp.inf)
    row_top = jnp.max(scores, axis=2, keepdims=True)
    row_total = jnp.sum(jnp.exp(scores - row_top), axis=2, keepdims=True)
    log_total = row_top + jnp.log(row_total)
    weights = jnp.exp(scores - log_total)
    weights_low = weights.astype(jnp.bfloat16)
    attended = jnp.einsum(
        "htk,khd->thd", weights_low, value_heads, preferred_element_type=jnp.float32
    ).astype(jnp.bfloat16)
    grad_rows = out_grad[0]
    attn_grad = lax.dot_general(
        grad_rows,
        lax.all_gather(out_weight, "fsdp", axis=0, tiled=True),
        (((1,), (1,)), ((), ())),
        preferred_element_type=jnp.float32,
    ).astype(jnp.bfloat16)
    attended_flat = attended.reshape(tokens_here, width_heads)
    weight_shard = lax.psum_scatter(
        lax.dot_general(
            attended_flat, grad_rows, (((0,), (0,)), ((), ())), preferred_element_type=jnp.float32
        ).astype(jnp.bfloat16),
        "fsdp",
        scatter_dimension=0,
        tiled=True,
    ).astype(jnp.float32)
    token_count = tokens_here * lax.axis_size("seq") * lax.axis_size("fsdp") * lax.axis_size("dp")
    weight_grad = (lax.psum(weight_shard, ("seq", "dp")) * (1.0 / math.sqrt(token_count))).astype(
        jnp.bfloat16
    )
    grad_heads = attn_grad.reshape(tokens_here, HEADS, HD)
    row_delta = jnp.einsum("thd,thd->ht", grad_heads, attended, preferred_element_type=jnp.float32)
    prob_grad = jnp.einsum(
        "thd,khd->htk", grad_heads, value_heads, preferred_element_type=jnp.float32
    )
    score_grad = (weights * (prob_grad - row_delta[:, :, None])).astype(jnp.bfloat16)
    query_grad = (
        jnp.einsum("htk,khd->thd", score_grad, key_heads, preferred_element_type=jnp.float32)
        * score_scale
    ).astype(jnp.bfloat16)
    query_all, grad_all = (
        lax.all_gather(query, "seq", axis=1, tiled=True),
        lax.all_gather(attn_grad[None], "seq", axis=1, tiled=True),
    )
    totals_all, deltas_all = (
        lax.all_gather(log_total[:, :, 0][None], "seq", axis=2, tiled=True),
        lax.all_gather(row_delta[None], "seq", axis=2, tiled=True),
    )
    local_keys = key[0].reshape(tokens_here, HEADS, HD)
    local_values = value[0].reshape(tokens_here, HEADS, HD)
    gathered_queries = query_all[0].reshape(-1, HEADS, HD)
    gathered_grads = grad_all[0].reshape(-1, HEADS, HD)
    back_scores = (
        jnp.einsum("khd,qhd->hkq", local_keys, gathered_queries, preferred_element_type=jnp.float32)
        * score_scale
    )
    back_allowed = query_pos[:, None] <= every_pos[None, :]
    back_scores = jnp.where(back_allowed[None], back_scores, -jnp.inf)
    back_weights = jnp.exp(back_scores - totals_all[0][:, None, :])
    back_low = back_weights.astype(jnp.bfloat16)
    back_prob_grad = jnp.einsum(
        "qhd,khd->hkq", gathered_grads, local_values, preferred_element_type=jnp.float32
    )
    back_score_grad = (back_weights * (back_prob_grad - deltas_all[0][:, None, :])).astype(
        jnp.bfloat16
    )
    key_grad = (
        jnp.einsum(
            "hkq,qhd->khd", back_score_grad, gathered_queries, preferred_element_type=jnp.float32
        )
        * score_scale
    ).astype(jnp.bfloat16)
    value_grad = jnp.einsum(
        "hkq,qhd->khd", back_low, gathered_grads, preferred_element_type=jnp.float32
    ).astype(jnp.bfloat16)
    return (
        query_grad.reshape(tokens_here, width_heads)[None],
        key_grad.reshape(tokens_here, width_heads)[None],
        value_grad.reshape(tokens_here, width_heads)[None],
        weight_grad,
    )


def solution(mesh):
    in_specs = (
        P(("fsdp", "dp"), "seq", None),
        P(("fsdp", "dp"), "seq", None),
        P(("fsdp", "dp"), "seq", None),
        P("fsdp", None),
        P(("fsdp", "dp"), "seq", None),
        P("seq"),
    )
    out_specs = (
        P(("fsdp", "dp"), "seq", None),
        P(("fsdp", "dp"), "seq", None),
        P(("fsdp", "dp"), "seq", None),
        P("fsdp", None),
    )
    return jax.shard_map(shards, mesh=mesh, in_specs=in_specs, out_specs=out_specs, check_vma=False)
```

profile of v0, /device:TPU:7, one launch (start us, length us, event | category | flops | bytes accessed | tf_op | source)
XLA Modules:
  0.0 382.1 jit_solution(4856913975927778064)
XLA Ops:
  7.2 0.0 copy-start
  7.2 0.0 all-gather.13.cloned.1.call-start
  7.2 0.7 all-gather.13.cloned.1.call-update
  7.9 0.0 all-gather.11.cloned.1.call-start
  8.0 0.7 all-gather.11.cloned.1.call-update
  8.7 0.0 all-gather.15.cloned.1.call-start
  8.7 0.7 all-gather.15.cloned.1.call-update
  9.4 0.0 all-gather.17.cloned.1.call-start
  9.4 0.5 all-gather.17.cloned.1.call-update
  10.0 0.0 all-gather.19.cloned.1.call-start
  10.0 1.2 dynamic-slice
  11.9 0.9 dynamic-update-slice
  12.8 6.4 %all-reduce = s32[8]{0:T(128)S(1)} all-reduce(s32[8]{0:T(128)S(1)} %dynamic-update-slice), channel_id=1, replica_groups=mesh['seq'=4,'fsdp'=2,'dp'=4] {'seq'}, use_global_device_ids=true, to_apply=%add | all-reduce | flops 8 | bytes 64
  19.2 0.1 iota_add_fusion
  19.3 0.1 add.65
  19.4 0.7 broadcast_multiply_fusion
  20.0 0.1 iota_add_fusion.1
  20.1 0.1 add.69
  20.2 1.1 copy.64
  21.3 45.3 %all-gather.13.cloned.1.call-done = bf16[1024,2048]{1,0:T(8,128)(2,1)} async-done(((bf16[512,2048]{1,0:T(8,128)(2,1)}), bf16[1024,2048]{1,0:T(8,128)(2,1)}) %all-gather.13.cloned.1.call-update) | async-done | bytes 4194320 | tf_op jit(solution)/shard_map/all_gather | solution.py:49
  66.6 0.0 copy-done
  66.6 4.5 %convolution_convert_fusion.1 = bf16[192,1024]{1,0:T(8,128)(2,1)} fusion(bf16[1024,2048]{1,0:T(8,128)(2,1)} %all-gather.13.cloned.1.call-done, bf16[1,192,2048]{2,1,0:T(8,128)(2,1)S(1)} %copy-done), kind=kOutput, calls=%fused_computation.38 | convolution fusion | flops 805502976 | bytes 5373952 | tf_op jit(solution)/shard_map/dot_general | solution.py:47
  71.1 0.0 all-gather.19.cloned.1.call-update
  71.1 0.0 reduce-scatter.2.cloned.1.call-start
  71.1 0.2 broadcast_compare_fusion
  71.4 34.7 %all-gather.11.cloned.1.call-done = bf16[1,768,1024]{2,1,0:T(8,128)(2,1)} async-done(((bf16[1,192,1024]{2,1,0:T(8,128)(2,1)}), bf16[1,768,1024]{2,1,0:T(8,128)(2,1)}) %all-gather.11.cloned.1.call-update) | async-done | bytes 1572880 | tf_op jit(solution)/shard_map/all_gather | solution.py:26
  106.1 1.7 copy.28
  107.8 0.0 copy-start.2
  107.8 35.8 %all-gather.15.cloned.1.call-done = bf16[1,768,1024]{2,1,0:T(8,128)(2,1)} async-done(((bf16[1,192,1024]{2,1,0:T(8,128)(2,1)}), bf16[1,768,1024]{2,1,0:T(8,128)(2,1)}) %all-gather.15.cloned.1.call-update) | async-done | bytes 1572880 | tf_op jit(solution)/shard_map/all_gather | solution.py:27
  143.7 2.6 copy.31
  146.3 1.0 fusion.3
  147.3 0.0 copy-done.2
  147.3 1.2 exponential_reduce_fusion
  148.6 0.1 copy.65
  148.6 0.1 bitcast_convert_fusion
  148.7 1.1 copy-done.3
  149.9 1.6 multiply_reduce_fusion
  151.5 0.0 copy-done.1
  151.5 3.4 convolution_convert_fusion
  154.9 0.0 reduce-scatter.2.cloned.1.call-update
  154.9 1.0 copy-done.4
  155.9 0.1 copy.66
  156.0 0.0 copy-done.5
  156.0 0.8 copy.67
  156.8 10.5 %all-gather.3 = f32[4,192,8]{1,2,0:T(8,128)S(1)} all-gather(f32[1,192,8]{1,2,0:T(8,128)S(1)} %bitcast.115), channel_id=2, replica_groups=mesh['seq'=4,'fsdp'=2,'dp'=4] {'seq'}, dimensions={0}, use_global_device_ids=true | all-gather | bytes 30720 | tf_op jit(solution)/shard_map/all_gather | solution.py:81
  167.4 0.1 reshape.140
  167.5 14.2 %all-gather.17.cloned.1.call-done = bf16[1,768,1024]{2,1,0:T(8,128)(2,1)} async-done(((bf16[1,192,1024]{2,1,0:T(8,128)(2,1)}), bf16[1,768,1024]{2,1,0:T(8,128)(2,1)}) %all-gather.17.cloned.1.call-update) | async-done | bytes 1572880 | tf_op jit(solution)/shard_map/all_gather | solution.py:77
  181.6 1.7 copy.37
  183.3 2.9 fusion.72
  186.3 6.3 %fusion.56 = bf16[192,8,128]{2,0,1:T(8,128)(2,1)} fusion(bf16[768,8,128]{0,2,1:T(8,128)(2,1)} %bitcast.105, f32[8,192,768]{2,1,0:T(8,128)} %copy-done.1, f32[8,192]{1,0:T(8,128)S(1)} %get-tuple-element.8, f32[8,192]{1,0:T(8,128)S(1)} %log_add_fusion, pred[192,768]{1,0:T(8,128)(4,1)S(1)} %get-tuple-element.5, bf16[768,8,128]{0,2,1:T(8,128)(2,1)} %bitcast.106, ...), kind=kOutput, calls=%fused_computation.40 | convolution fusion | flops 611450880 | bytes 8810496 | tf_op jit(solution)/shard_map/htk,khd->thd/dot_general | solution.py:73
  192.5 1.3 copy.36
  193.8 0.9 broadcast_in_dim_reshape.6
  194.7 10.7 %all-gather.4 = f32[4,192,8]{1,2,0:T(8,128)S(1)} all-gather(f32[1,192,8]{1,2,0:T(8,128)S(1)} %bitcast.119), channel_id=4, replica_groups=mesh['seq'=4,'fsdp'=2,'dp'=4] {'seq'}, dimensions={0}, use_global_device_ids=true | all-gather | bytes 30720 | tf_op jit(solution)/shard_map/all_gather | solution.py:82
  205.4 0.1 reshape.142
  205.5 14.6 %all-gather.19.cloned.1.call-done = bf16[768,1024]{1,0:T(8,128)(2,1)} async-done(((bf16[192,1024]{1,0:T(8,128)(2,1)}), bf16[768,1024]{1,0:T(8,128)(2,1)}) %all-gather.19.cloned.1.call-update) | async-done | bytes 1572880 | tf_op jit(solution)/shard_map/all_gather | solution.py:78
  220.1 4.8 %fusion.51 = bf16[192,8,128]{2,0,1:T(8,128)(2,1)S(1)} fusion(bf16[768,8,128]{0,2,1:T(8,128)(2,1)S(1)} %bitcast.103, f32[8,192,768]{2,1,0:T(8,128)} %fusion.72, f32[8,768]{1,0:T(8,128)S(1)} %bitcast.118, f32[8,768]{1,0:T(8,128)S(1)} %bitcast.116, pred[192,768]{1,0:T(8,128)(4,1)S(1)} %get-tuple-element.4, bf16[192,8,128]{2,1,0:T(8,128)(2,1)S(1)} %bitcast.114, ...), kind=kOutput, calls=%fused_computation.39 | convolution fusion | flops 611450880 | bytes 8847360 | tf_op jit(solution)/shard_map/hkq,qhd->khd/dot_general | solution.py:103
  224.9 0.3 copy.45
  225.2 0.9 broadcast_in_dim_reshape.14
  226.1 4.9 %fusion.57 = bf16[192,8,128]{2,0,1:T(8,128)(2,1)S(1)} fusion(f32[8,192,768]{2,1,0:T(8,128)} %fusion.72, f32[8,768]{1,0:T(8,128)S(1)} %bitcast.117, pred[192,768]{1,0:T(8,128)(4,1)S(1)} %get-tuple-element.4, bf16[768,1024]{1,0:T(8,128)(2,1)} %all-gather.19.cloned.1.call-done), kind=kOutput, calls=%fused_computation.41 | convolution fusion | flops 306905088 | bytes 6856704 | tf_op jit(solution)/shard_map/hkq,qhd->khd/dot_general | solution.py:108
  231.1 0.3 copy.47
  231.3 0.9 broadcast_in_dim_reshape.15
  232.3 42.4 %reduce-scatter.2.cloned.1.call-done = bf16[512,2048]{1,0:T(8,128)(2,1)} async-done(((bf16[1024,2048]{1,0:T(8,128)(2,1)}), bf16[512,2048]{1,0:T(8,128)(2,1)}) %reduce-scatter.2.cloned.1.call-update) | async-done | bytes 2097168 | tf_op jit(solution)/shard_map/reduce_scatter | solution.py:54
  274.7 96.6 %all-reduce.2 = f32[512,2048]{1,0:T(8,128)} all-reduce(bf16[512,2048]{1,0:T(8,128)(2,1)} %reduce-scatter.2.cloned.1.call-done), channel_id=1, replica_groups=mesh['seq'=4,'fsdp'=2,'dp'=4] {'seq','dp'}, use_global_device_ids=true, to_apply=%region_3.4 | all-reduce | flops 1048576 | bytes 6291456 | tf_op jit(solution)/shard_map/psum | solution.py:63
  371.2 4.0 %multiply_convert_fusion.1 = bf16[512,2048]{1,0:T(8,128)(2,1)} fusion(f32[512,2048]{1,0:T(8,128)} %all-reduce.2), kind=kLoop, calls=%fused_computation.7 | loop fusion | flops 2097152 | bytes 6291456 | tf_op jit(solution)/shard_map/convert_element_type | solution.py:63
  (13 shorter events, 0.1 us)
Async XLA Ops:
  7.2 59.4 %copy-start = (bf16[1,192,2048]{2,1,0:T(8,128)(2,1)S(1)}, bf16[1,192,2048]{2,1,0:T(8,128)(2,1)}, u32[]{:S(2)}) copy-start(bf16[1,192,2048]{2,1,0:T(8,128)(2,1)} %param.10) | copy-start | bytes 2359300
  7.2 59.4 %all-gather.13.cloned.1.call-start = ((), (), s32[]{:S(2)}) async-start(), calls=%async_computation.2 | async-start | bytes 6291456 | tf_op jit(solution)/shard_map/all_gather | solution.py:49
  7.9 98.2 %all-gather.11.cloned.1.call-start = ((), (), s32[]{:S(2)}) async-start(), calls=%async_computation.1 | async-start | bytes 1966080 | tf_op jit(solution)/shard_map/all_gather | solution.py:26
  8.7 135.0 %all-gather.15.cloned.1.call-start = ((), (), s32[]{:S(2)}) async-start(), calls=%async_computation.3 | async-start | bytes 1966080 | tf_op jit(solution)/shard_map/all_gather | solution.py:27
  9.4 172.2 %all-gather.17.cloned.1.call-start = ((), (), s32[]{:S(2)}) async-start(), calls=%async_computation.4 | async-start | bytes 1966080 | tf_op jit(solution)/shard_map/all_gather | solution.py:77
  10.0 210.1 %all-gather.19.cloned.1.call-start = ((), (), s32[]{:S(2)}) async-start(), calls=%async_computation.6 | async-start | bytes 1966080 | tf_op jit(solution)/shard_map/all_gather | solution.py:78
  71.1 203.6 %reduce-scatter.2.cloned.1.call-start = ((), (), s32[]{:S(2)}) async-start(), calls=%async_computation.5 | async-start | bytes 6291456 | tf_op jit(solution)/shard_map/reduce_scatter | solution.py:54
  107.8 39.5 %copy-start.2 = (bf16[1,768,1024]{1,2,0:T(8,128)(2,1)}, bf16[1,768,1024]{1,2,0:T(8,128)(2,1)S(1)}, u32[]{:S(2)}) copy-start(bf16[1,768,1024]{1,2,0:T(8,128)(2,1)S(1)} %copy.28) | copy-start | bytes 4718596
  146.2 2.3 copy-start.6
  147.3 4.2 %copy-start.1 = (f32[8,192,768]{2,1,0:T(8,128)}, f32[8,192,768]{2,1,0:T(8,128)S(1)}, u32[]{:S(2)}) copy-start(f32[8,192,768]{2,1,0:T(8,128)S(1)} %get-tuple-element.7) | copy-start | bytes 14155780
  147.3 2.6 copy-start.3
  154.9 1.0 copy-start.4
  154.9 1.1 copy-start.5
  186.3 33.8 %copy-start.7 = (bf16[24,8,8,128]{3,2,1,0:T(8,128)(2,1)S(1)}, bf16[24,8,8,128]{3,2,1,0:T(8,128)(2,1)}, u32[]{:S(2)}) copy-start(bf16[24,8,8,128]{3,2,1,0:T(8,128)(2,1)} %copy.67) | copy-start | bytes 1179652
Sparse Core Ops, SparseCore 0:
  9.6 56.9 all-gather.12
  68.2 37.8 all-gather.10
  107.7 35.9 all-gather.14
  145.1 36.4 all-gather.16
  183.6 36.4 all-gather.18
  222.3 52.3 reduce-scatter.1
where the time goes:
time: 385 us; the launch traced here: 382 us
  waiting for transfers between devices  190 us (49%)
  blocking collectives  124 us (32%)
  matrix products  29.5 us (8%)
  local copies, waits for them, and re-layouts  17.2 us (4%)
  between operations  14.9 us (4%)
  other arithmetic  6.4 us (2%)
    psum x1, blocking collectives, shards(): lax.psum(weight_shard, ('seq', 'dp')) * (1.0 / math.sqrt(token_count))  96.6 us
    all_gather x1, waiting for transfers between devices, shards(): lax.all_gather(out_weight, 'fsdp', axis=0, tiled=True)  45.3 us
    reduce_scatter x1, waiting for transfers between devices, shards(): lax.psum_scatter(lax.dot_general(attended_flat, grad_rows, (((0,), (0,)),...  42.4 us
    all_gather x1, waiting for transfers between devices, shards(): lax.all_gather(value, 'seq', axis=1, tiled=True)  35.8 us
    all_gather x1, waiting for transfers between devices, shards(): lax.all_gather(key, 'seq', axis=1, tiled=True)  34.7 us
    all_gather x1, waiting for transfers between devices, shards(): lax.all_gather(attn_grad[None], 'seq', axis=1, tiled=True)  14.6 us
    all_gather x1, waiting for transfers between devices, shards(): lax.all_gather(query, 'seq', axis=1, tiled=True)  14.2 us
    all_gather x1, blocking collectives, shards(): lax.all_gather(row_delta[None], 'seq', axis=2, tiled=True)  10.7 us
  transfers between devices with their start and end apart: 6, of which 6 were waited for; matrix products, arithmetic and copies ran while one was open for 12% of the time, Pallas kernels for 0%

commit v1 on v0

--- a/solution.py
+++ b/solution.py
@@ -1,12 +1,18 @@
+import functools
 import math
 
 import jax
 import jax.numpy as jnp
 from jax import lax
+from jax.experimental import pallas as pl
+from jax.experimental.pallas import tpu as pltpu
 from jax.sharding import PartitionSpec as P
 
 HEADS = 8
 HD = 128
+MESH = pl.DeviceIdType.MESH
+F32 = jnp.float32
+BF16 = jnp.bfloat16
 
 
 def positions_of(block_list, block_rows):
@@ -116,6 +122,343 @@
     )
 
 
+def contract(a, b, da, db):
+    return lax.dot_general(a, b, (((da,), (db,)), ((), ())), preferred_element_type=F32)
+
+
+def fused_kernel(
+    sizes, blocks_ref, q_ref, k_ref, v_ref, w_ref, og_ref, dq_ref, dk_ref, dv_ref, dw_ref,
+    idg, posc, posr, qg, kg, vg, ogall, ws, dos, dog, prob, atts, attg, dqs, dks, dvs, dka, dva,
+    wacc, wpart, wrecv, wfin,
+    id_s, id_r, in_s, in_r, og_s, og_r, w_sem, do_s, do_r, at_s, at_r, out_s, out_r,
+    ws_s, ws_r, wf_s, wf_r, wx_s, wc_s,
+):
+    nz, nf, nd, blocks = sizes
+    rows = q_ref.shape[0]
+    length = rows * nz
+    block_rows = length // blocks
+    local_heads = HEADS // nz
+    cut = HD // nz
+    token_count = length * nf * nd
+    scale = 1.0 / math.sqrt(HD)
+    z, f, d = lax.axis_index("seq"), lax.axis_index("fsdp"), lax.axis_index("dp")
+    p = f * nd + d
+    plane = nf * nd
+    total = nz * plane
+    me = z * plane + p
+    pending = []
+
+    def at(zz, ff, dd):
+        return {"seq": zz, "fsdp": ff, "dp": dd}
+
+    def put(src, dst, ssem, rsem, target, same=None):
+        copy = pltpu.make_async_remote_copy(
+            src_ref=src, dst_ref=dst, send_sem=ssem, recv_sem=rsem,
+            device_id=target, device_id_type=MESH,
+        )
+        if same is None:
+            copy.start()
+        else:
+            @pl.when(jnp.logical_not(same))
+            def _():
+                copy.start()
+
+            @pl.when(same)
+            def _():
+                pltpu.make_async_copy(src, dst, rsem).start()
+        pending.append((copy, same))
+
+    def keep(src, dst, sem):
+        pltpu.make_async_copy(src, dst, sem).start()
+
+    def arrived(dst, sem):
+        pltpu.make_async_copy(dst, dst, sem).wait()
+
+    def band(i):
+        return pl.ds(pl.multiple_of(i * rows, rows), rows)
+
+    def head_cols(h):
+        return pl.ds(pl.multiple_of(h * HD, HD), HD)
+
+    barrier = pltpu.get_barrier_semaphore()
+
+    def greet(i, c):
+        t = lax.rem(me + i, total)
+        pl.semaphore_signal(
+            barrier, inc=1, device_id=at(t // plane, (t // nd) % nf, t % nd), device_id_type=MESH
+        )
+        return c
+
+    keep(w_ref.at[pl.ds(pl.multiple_of(d * HD, HD), HD)], ws, w_sem)
+    keep(og_ref, ogall.at[p], og_r.at[p, 0])
+    lax.fori_loop(1, total, greet, 0)
+    pl.semaphore_wait(barrier, total - 1)
+
+    dx = (d + nd // 2) % nd
+    dc = d + 1 - 2 * (d % 2)
+    fy = 1 - f
+    other = lambda i: i + 1 - 2 * (i % 2)
+    py, px, pxy = fy * nd + d, f * nd + dx, fy * nd + dx
+    half = rows // 2
+    halves = (pl.ds(0, half), pl.ds(half, half))
+    put(og_ref, ogall.at[p], og_s.at[0], og_r.at[p, 0], at(z, fy, d))
+    put(og_ref, ogall.at[p], og_s.at[1], og_r.at[p, 0], at(z, f, dx))
+    for o in range(1, nz):
+        t = (z + o) % nz
+        put(blocks_ref, idg.at[z], id_s.at[o], id_r.at[z], at(t, f, d))
+    triples = ((k_ref, kg), (q_ref, qg), (v_ref, vg))
+    for j in range(local_heads):
+        for n, (src, dst) in enumerate(triples):
+            for o in range(nz):
+                t = (z + o) % nz
+                piece, place = src.at[:, head_cols(t * local_heads + j)], dst.at[j, band(z)]
+                if o == 0:
+                    keep(piece, place, in_r.at[n, j, z])
+                else:
+                    put(piece, place, in_s.at[n, j, o], in_r.at[n, j, z], at(t, f, d))
+        if j == 0:
+            put(og_ref, ogall.at[p], og_s.at[2], og_r.at[p, 0], at(z, f, dc))
+
+    head = f * nd + d
+    head_z, head_j = head // local_heads, head % local_heads
+
+    def grad_of(i):
+        dos[i] = contract(ogall[i], ws[...], 1, 1).astype(BF16)
+        put(
+            dos.at[i], dog.at[head_j, band(z)], do_s.at[len(grads)], do_r.at[head_j, z],
+            at(head_z, i // nd, i % nd),
+            jnp.logical_and(head_z == z, p == i) if len(grads) == 0 else None,
+        )
+        grads.append(i)
+
+    grads = []
+    arrived(ws, w_sem)
+    arrived(ogall.at[p], og_r.at[p, 0])
+    grad_of(p)
+
+    ids = blocks_ref[...]
+    for o in range(1, nz):
+        t = (z + o) % nz
+        arrived(idg.at[t], id_r.at[t])
+        ids = ids + idg[t]
+    along = lax.broadcasted_iota(jnp.int32, posr.shape, 1)
+    down = lax.broadcasted_iota(jnp.int32, posc.shape, 0)
+    row_pos = jnp.zeros(posr.shape, jnp.int32)
+    col_pos = jnp.zeros(posc.shape, jnp.int32)
+    for b in range(blocks):
+        low, shift = b * block_rows, ids[b : b + 1, :1] * block_rows - b * block_rows
+        row_pos = jnp.where((along >= low) & (along < low + block_rows), along + shift, row_pos)
+        col_pos = jnp.where((down >= low) & (down < low + block_rows), down + shift, col_pos)
+    posr[...] = row_pos
+    posc[...] = col_pos
+
+    def forward(j):
+        for n, (_, dst) in enumerate(triples):
+            for o in range(nz):
+                arrived(dst.at[j, band(o)], in_r.at[n, j, o])
+
+        def step(b, c):
+            r = band(b)
+            s = contract(qg[j, r, :], kg[j], 1, 1) * scale
+            s = jnp.where(posr[0:1, :] <= posc[r, :][:, :1], s, -jnp.inf)
+            e = jnp.exp(s - jnp.max(s, axis=1, keepdims=True))
+            w = e * (1.0 / jnp.sum(e, axis=1, keepdims=True))
+            prob[j, r, :] = w
+            atts[j, r, :] = contract(w.astype(BF16), vg[j], 1, 0).astype(BF16)
+            return c
+
+        lax.fori_loop(0, nz, step, 0)
+        h = z * local_heads + j
+        hf, hd = h // nd, h % nd
+        for o in range(nz):
+            t = (z + o) % nz
+            put(
+                atts.at[j, band(t)], attg.at[p], at_s.at[j, o], at_r.at[p], at(t, hf, hd),
+                (h == p) if o == 0 else None,
+            )
+
+    def backward(j):
+        for o in range(nz):
+            arrived(dog.at[j, band(o)], do_r.at[j, o])
+        dka[...] = jnp.zeros(dka.shape, F32)
+        dva[...] = jnp.zeros(dva.shape, F32)
+
+        def step(b, c):
+            r = band(b)
+            do = dog[j, r, :]
+            w = prob[j, r, :]
+            delta = jnp.sum(do.astype(F32) * atts[j, r, :].astype(F32), axis=1, keepdims=True)
+            ds = (w * (contract(do, vg[j], 1, 1) - delta)).astype(BF16)
+            dqs[j, r, :] = (contract(ds, kg[j], 1, 0) * scale).astype(BF16)
+            dka[...] += contract(ds, qg[j, r, :], 0, 0)
+            dva[...] += contract(w.astype(BF16), do, 0, 0)
+            return c
+
+        lax.fori_loop(0, nz, step, 0)
+        dks[j] = (dka[...] * scale).astype(BF16)
+        dvs[j] = dva[...].astype(BF16)
+        h = z * local_heads + j
+        for n, (src, dst) in enumerate(((dqs, dq_ref), (dks, dk_ref), (dvs, dv_ref))):
+            for o in range(1, nz + 1):
+                t = (z + o) % nz
+                piece, place = src.at[j, band(t)], dst.at[:, head_cols(h)]
+                if o == nz:
+                    keep(piece, place, out_r.at[n, h])
+                else:
+                    put(piece, place, out_s.at[n, j, o], out_r.at[n, h], at(t, f, d))
+
+    forward(0)
+
+    arrived(ogall.at[py], og_r.at[py, 0])
+    put(ogall.at[py, halves[0]], ogall.at[py, halves[0]], og_s.at[3], og_r.at[py, 0], at(z, f, dx))
+    put(ogall.at[py], ogall.at[py], og_s.at[4], og_r.at[py, 0], at(z, f, dc))
+    arrived(ogall.at[px], og_r.at[px, 0])
+    put(ogall.at[px, halves[1]], ogall.at[px, halves[1]], og_s.at[5], og_r.at[px, 1], at(z, fy, d))
+    put(ogall.at[px], ogall.at[px], og_s.at[6], og_r.at[px, 0], at(z, f, dc))
+    grad_of(py)
+    grad_of(px)
+    arrived(ogall.at[other(p)], og_r.at[other(p), 0])
+    grad_of(other(p))
+    for i in (other(py), other(px)):
+        arrived(ogall.at[i], og_r.at[i, 0])
+        grad_of(i)
+
+    forward(1)
+
+    for n in range(2):
+        arrived(ogall.at[pxy, halves[n]], og_r.at[pxy, n])
+        put(
+            ogall.at[pxy, halves[n]], ogall.at[pxy, halves[n]], og_s.at[7 + n], og_r.at[pxy, n],
+            at(z, f, dc),
+        )
+    grad_of(pxy)
+    for n in range(2):
+        arrived(ogall.at[other(pxy), halves[n]], og_r.at[other(pxy), n])
+    grad_of(other(pxy))
+
+    backward(0)
+
+    for i in range(plane):
+        arrived(attg.at[i], at_r.at[i])
+    wacc[...] = jnp.zeros(wacc.shape, F32)
+
+    def add(i, c):
+        wacc[...] += contract(attg[i], ogall[i], 0, 0)
+        return c
+
+    lax.fori_loop(0, plane, add, 0)
+    wpart[...] = wacc[...].astype(BF16)
+
+    def cut_rows(i):
+        return pl.ds(pl.multiple_of(i * cut, cut), cut)
+
+    for o in range(1, nz):
+        t = (z + o) % nz
+        put(wpart.at[cut_rows(t)], wrecv.at[z], ws_s.at[o], ws_r.at[z], at(t, f, d))
+
+    backward(1)
+
+    share = wacc[cut_rows(z), :]
+    for o in range(1, nz):
+        t = (z + o) % nz
+        arrived(wrecv.at[t], ws_r.at[t])
+        share = share + wrecv[t].astype(F32)
+    wfin[...] = (share * (1.0 / math.sqrt(token_count))).astype(BF16)
+
+    def final(dd, zz):
+        return dw_ref.at[pl.ds(pl.multiple_of(dd * HD + zz * cut, cut), cut)]
+
+    for o in range(1, nz):
+        put(wfin, final(d, z), wf_s.at[o], wf_r.at[d, z], at((z + o) % nz, f, d))
+    put(wfin, final(d, z), wx_s.at[0], wf_r.at[d, z], at(z, f, dx))
+    put(wfin, final(d, z), wc_s.at[0, 0], wf_r.at[d, z], at(z, f, dc))
+    keep(wfin, final(d, z), wf_r.at[d, z])
+    for o in range(1, nz):
+        t = (z + o) % nz
+        arrived(final(d, t), wf_r.at[d, t])
+        put(final(d, t), final(d, t), wx_s.at[o], wf_r.at[d, t], at(z, f, dx))
+        put(final(d, t), final(d, t), wc_s.at[0, o], wf_r.at[d, t], at(z, f, dc))
+    for o in range(nz):
+        t = (z + o) % nz
+        arrived(final(dx, t), wf_r.at[dx, t])
+        put(final(dx, t), final(dx, t), wc_s.at[1, o], wf_r.at[dx, t], at(z, f, dc))
+    dxc = other(dx)
+    arrived(final(d, z), wf_r.at[d, z])
+    for dd in (dc, dxc):
+        for o in range(nz):
+            arrived(final(dd, o), wf_r.at[dd, o])
+    for n, dst in enumerate((dq_ref, dk_ref, dv_ref)):
+        for h in range(HEADS):
+            arrived(dst.at[:, pl.ds(h * HD, HD)], out_r.at[n, h])
+    for copy, same in pending:
+        if same is None:
+            copy.wait_send()
+        else:
+            @pl.when(jnp.logical_not(same))
+            def _(copy=copy):
+                copy.wait_send()
+
+
+def fused(mesh, query, key, value, out_weight, out_grad, block_ids):
+    nz, nf, nd = mesh.shape["seq"], mesh.shape["fsdp"], mesh.shape["dp"]
+    rows, width = query.shape[1], query.shape[2]
+    model = out_grad.shape[2]
+    here = block_ids.shape[0]
+    blocks = here * nz
+    length = rows * nz
+    plane = nf * nd
+    local_heads = HEADS // nz
+    cut = HD // nz
+    first = lax.axis_index("seq") * here
+    index = jnp.arange(blocks, dtype=jnp.int32)
+    spread = sum(jnp.where(index == first + i, block_ids[i], 0) for i in range(here))
+    tile = jnp.broadcast_to(spread[:, None], (blocks, 128))
+    dma = pltpu.SemaphoreType.DMA
+    vm = pltpu.VMEM
+    heads_all = (local_heads, length, HD)
+    grads = jax.ShapeDtypeStruct((rows, width), BF16)
+    anyspec = pl.BlockSpec(memory_space=pl.ANY)
+    dq, dk, dv, dw = pl.pallas_call(
+        functools.partial(fused_kernel, (nz, nf, nd, blocks)),
+        out_shape=(grads, grads, grads, jax.ShapeDtypeStruct(out_weight.shape, BF16)),
+        in_specs=[pl.BlockSpec(memory_space=pltpu.VMEM)] + [anyspec] * 5,
+        out_specs=(anyspec,) * 4,
+        scratch_shapes=[
+            vm((nz, blocks, 128), jnp.int32),
+            vm((length, 128), jnp.int32),
+            vm((8, length), jnp.int32),
+            vm(heads_all, BF16), vm(heads_all, BF16), vm(heads_all, BF16),
+            vm((plane, rows, model), BF16),
+            vm((HD, model), BF16),
+            vm((plane, rows, HD), BF16),
+            vm(heads_all, BF16),
+            vm((local_heads, length, length), F32),
+            vm(heads_all, BF16),
+            vm((plane, rows, HD), BF16),
+            vm(heads_all, BF16), vm(heads_all, BF16), vm(heads_all, BF16),
+            vm((length, HD), F32), vm((length, HD), F32),
+            vm((HD, model), F32),
+            vm((HD, model), BF16),
+            vm((nz, cut, model), BF16),
+            vm((cut, model), BF16),
+            dma((nz,)), dma((nz,)),
+            dma((3, local_heads, nz)), dma((3, local_heads, nz)),
+            dma((9,)), dma((plane, 2)),
+            dma,
+            dma((plane,)), dma((local_heads, nz)),
+            dma((local_heads, nz)), dma((plane,)),
+            dma((3, local_heads, nz)), dma((3, HEADS)),
+            dma((nz,)), dma((nz,)),
+            dma((nz,)), dma((nd, nz)),
+            dma((nz,)), dma((2, nz)),
+        ],
+        compiler_params=pltpu.CompilerParams(
+            collective_id=0, has_side_effects=True, vmem_limit_bytes=48 * 1024 * 1024
+        ),
+    )(tile, query[0], key[0], value[0], out_weight, out_grad[0])
+    return dq[None], dk[None], dv[None], dw
+
+
 def solution(mesh):
     in_specs = (
         P(("fsdp", "dp"), "seq", None),
@@ -131,4 +474,7 @@
         P(("fsdp", "dp"), "seq", None),
         P("fsdp", None),
     )
-    return jax.shard_map(shards, mesh=mesh, in_specs=in_specs, out_specs=out_specs, check_vma=False)
+    part = shards
+    if mesh.shape["fsdp"] == 2 and mesh.shape["dp"] == 4 and mesh.shape["seq"] == 4:
+        part = functools.partial(fused, mesh)
+    return jax.shard_map(part, mesh=mesh, in_specs=in_specs, out_specs=out_specs, check_vma=False)

time: 385 us -> 132 us (0.34)
  the two profiles are of different devices: /device:TPU:7 before, /device:TPU:9 now
where the time goes in v1:
time: 132 us
  Pallas kernels  120 us (91%)
  local copies, waits for them, and re-layouts  9.06 us (7%)
    pallas_call x1, Pallas kernels, fused(): pl.pallas_call(functools.partial(fused_kernel, (nz, nf, nd, blocks)), out...  120 us
    unnamed x12, local copies, waits for them, and re-layouts  7.68 us

profile of v1, /device:TPU:9, one launch (start us, length us, event | category | flops | bytes accessed | tf_op | source)
XLA Modules:
  0.0 131.5 jit_solution(9222527504016809556)
XLA Ops:
  0.6 1.3 fusion.1
  1.9 1.3 fusion
  3.3 0.1 broadcast_in_dim.30.blocks_ref
  3.3 0.0 copy-start
  3.3 1.1 copy-done
  4.5 0.0 copy-start.1
  4.5 1.0 copy-done.1
  5.5 0.0 copy-start.2
  5.5 1.0 copy-done.2
  6.4 0.0 copy-start.3
  6.5 1.0 copy-done.3
  7.4 120.5 %shard_map.93 = (bf16[192,1024]{1,0:T(8,128)(2,1)S(1)}, bf16[192,1024]{1,0:T(8,128)(2,1)S(1)}, bf16[192,1024]{1,0:T(8,128)(2,1)S(1)}, bf16[512,2048]{1,0:T(8,128)(2,1)S(1)}) custom-call(s32[8,128]{1,0:T(8,128)S(1)} %broadcast_in_dim.30.blocks_ref, bf16[192,1024]{1,0:T(8,128)(2,1)S(1)} %bitcast.10, bf16[192,1024]{1,0:T(8,128)(2,1)S(1)} %bitcast.11, ...), custom_call_target="tpu_custom_call" | custom-call | tf_op jit(solution)/shard_map/pallas_call | solution.py:421
  127.9 0.7 copy.14
  128.7 0.7 copy.15
  129.4 0.7 copy.16
  130.2 1.3 %copy.17 = bf16[512,2048]{1,0:T(8,128)(2,1)} copy(bf16[512,2048]{1,0:T(8,128)(2,1)S(1)} %get-tuple-element.21) | data formatting | bytes 4194304
Async XLA Ops:
  3.3 1.1 copy-start
  4.5 1.0 copy-start.1
  5.5 1.0 copy-start.2
  6.4 1.0 copy-start.3

commit v2 on v1

--- a/solution.py
+++ b/solution.py
@@ -127,8 +127,8 @@
 
 
 def fused_kernel(
-    sizes, blocks_ref, q_ref, k_ref, v_ref, w_ref, og_ref, dq_ref, dk_ref, dv_ref, dw_ref,
-    idg, posc, posr, qg, kg, vg, ogall, ws, dos, dog, prob, atts, attg, dqs, dks, dvs, dka, dva,
+    sizes, ids_ref, q_ref, k_ref, v_ref, w_ref, og_ref, dq_ref, dk_ref, dv_ref, dw_ref,
+    blocks_ref, idg, posc, posr, qg, kg, vg, ogall, ws, dos, dog, prob, atts, attg, dqs, dks, dvs, dka, dva,
     wacc, wpart, wrecv, wfin,
     id_s, id_r, in_s, in_r, og_s, og_r, w_sem, do_s, do_r, at_s, at_r, out_s, out_r,
     ws_s, ws_r, wf_s, wf_r, wx_s, wc_s,
@@ -189,6 +189,12 @@
         )
         return c
 
+    here = blocks // nz
+    line = lax.broadcasted_iota(jnp.int32, blocks_ref.shape, 0)
+    tile = jnp.zeros(blocks_ref.shape, jnp.int32)
+    for i in range(here):
+        tile = jnp.where(line == z * here + i, ids_ref[i], tile)
+    blocks_ref[...] = tile
     keep(w_ref.at[pl.ds(pl.multiple_of(d * HD, HD), HD)], ws, w_sem)
     keep(og_ref, ogall.at[p], og_r.at[p, 0])
     lax.fori_loop(1, total, greet, 0)
@@ -265,17 +271,25 @@
             w = e * (1.0 / jnp.sum(e, axis=1, keepdims=True))
             prob[j, r, :] = w
             atts[j, r, :] = contract(w.astype(BF16), vg[j], 1, 0).astype(BF16)
+
+        h = z * local_heads + j
+
+        def give(o):
+            t = (z + o) % nz
+            return pltpu.make_async_remote_copy(
+                src_ref=atts.at[j, band(t)], dst_ref=attg.at[p], send_sem=at_s.at[j, o],
+                recv_sem=at_r.at[p], device_id=at(t, h // nd, h % nd), device_id_type=MESH,
+            )
+
+        def turn(o, c):
+            step((z + o) % nz, c)
+            give(o).start()
             return c
 
-        lax.fori_loop(0, nz, step, 0)
-        h = z * local_heads + j
-        hf, hd = h // nd, h % nd
-        for o in range(nz):
-            t = (z + o) % nz
-            put(
-                atts.at[j, band(t)], attg.at[p], at_s.at[j, o], at_r.at[p], at(t, hf, hd),
-                (h == p) if o == 0 else None,
-            )
+        lax.fori_loop(1, nz, turn, 0)
+        step(z, 0)
+        pending.extend((give(o), None) for o in range(1, nz))
+        put(atts.at[j, band(z)], attg.at[p], at_s.at[j, 0], at_r.at[p], at(z, h // nd, h % nd), h == p)
 
     def backward(j):
         for o in range(nz):
@@ -292,13 +306,29 @@
             dqs[j, r, :] = (contract(ds, kg[j], 1, 0) * scale).astype(BF16)
             dka[...] += contract(ds, qg[j, r, :], 0, 0)
             dva[...] += contract(w.astype(BF16), do, 0, 0)
+
+        h = z * local_heads + j
+
+        def give(o):
+            t = (z + o) % nz
+            return pltpu.make_async_remote_copy(
+                src_ref=dqs.at[j, band(t)], dst_ref=dq_ref.at[:, head_cols(h)],
+                send_sem=out_s.at[0, j, o], recv_sem=out_r.at[0, h], device_id=at(t, f, d),
+                device_id_type=MESH,
+            )
+
+        def turn(o, c):
+            step((z + o) % nz, c)
+            give(o).start()
             return c
 
-        lax.fori_loop(0, nz, step, 0)
+        lax.fori_loop(1, nz, turn, 0)
+        step(z, 0)
+        pending.extend((give(o), None) for o in range(1, nz))
+        keep(dqs.at[j, band(z)], dq_ref.at[:, head_cols(h)], out_r.at[0, h])
         dks[j] = (dka[...] * scale).astype(BF16)
         dvs[j] = dva[...].astype(BF16)
-        h = z * local_heads + j
-        for n, (src, dst) in enumerate(((dqs, dq_ref), (dks, dk_ref), (dvs, dv_ref))):
+        for n, (src, dst) in ((1, (dks, dk_ref)), (2, (dvs, dv_ref))):
             for o in range(1, nz + 1):
                 t = (z + o) % nz
                 piece, place = src.at[j, band(t)], dst.at[:, head_cols(h)]
@@ -336,8 +366,6 @@
         arrived(ogall.at[other(pxy), halves[n]], og_r.at[other(pxy), n])
     grad_of(other(pxy))
 
-    backward(0)
-
     for i in range(plane):
         arrived(attg.at[i], at_r.at[i])
     wacc[...] = jnp.zeros(wacc.shape, F32)
@@ -356,7 +384,7 @@
         t = (z + o) % nz
         put(wpart.at[cut_rows(t)], wrecv.at[z], ws_s.at[o], ws_r.at[z], at(t, f, d))
 
-    backward(1)
+    backward(0)
 
     share = wacc[cut_rows(z), :]
     for o in range(1, nz):
@@ -373,6 +401,9 @@
     put(wfin, final(d, z), wx_s.at[0], wf_r.at[d, z], at(z, f, dx))
     put(wfin, final(d, z), wc_s.at[0, 0], wf_r.at[d, z], at(z, f, dc))
     keep(wfin, final(d, z), wf_r.at[d, z])
+
+    backward(1)
+
     for o in range(1, nz):
         t = (z + o) % nz
         arrived(final(d, t), wf_r.at[d, t])
@@ -409,10 +440,6 @@
     plane = nf * nd
     local_heads = HEADS // nz
     cut = HD // nz
-    first = lax.axis_index("seq") * here
-    index = jnp.arange(blocks, dtype=jnp.int32)
-    spread = sum(jnp.where(index == first + i, block_ids[i], 0) for i in range(here))
-    tile = jnp.broadcast_to(spread[:, None], (blocks, 128))
     dma = pltpu.SemaphoreType.DMA
     vm = pltpu.VMEM
     heads_all = (local_heads, length, HD)
@@ -421,9 +448,10 @@
     dq, dk, dv, dw = pl.pallas_call(
         functools.partial(fused_kernel, (nz, nf, nd, blocks)),
         out_shape=(grads, grads, grads, jax.ShapeDtypeStruct(out_weight.shape, BF16)),
-        in_specs=[pl.BlockSpec(memory_space=pltpu.VMEM)] + [anyspec] * 5,
+        in_specs=[pl.BlockSpec(memory_space=pltpu.SMEM)] + [anyspec] * 5,
         out_specs=(anyspec,) * 4,
         scratch_shapes=[
+            vm((blocks, 128), jnp.int32),
             vm((nz, blocks, 128), jnp.int32),
             vm((length, 128), jnp.int32),
             vm((8, length), jnp.int32),
@@ -453,9 +481,9 @@
             dma((nz,)), dma((2, nz)),
         ],
         compiler_params=pltpu.CompilerParams(
-            collective_id=0, has_side_effects=True, vmem_limit_bytes=48 * 1024 * 1024
+            collective_id=0, has_side_effects=True, vmem_limit_bytes=60 * 1024 * 1024
         ),
-    )(tile, query[0], key[0], value[0], out_weight, out_grad[0])
+    )(block_ids, query[0], key[0], value[0], out_weight, out_grad[0])
     return dq[None], dk[None], dv[None], dw
 
 

time: 132 us -> 121 us (0.917)
  the two profiles are of different devices: /device:TPU:9 before, /device:TPU:11 now
where the time goes in v2:
time: 121 us
  Pallas kernels  114 us (94%)
  local copies, waits for them, and re-layouts  6.77 us (6%)
    pallas_call x1, Pallas kernels, fused(): pl.pallas_call(functools.partial(fused_kernel, (nz, nf, nd, blocks)), out...  114 us
    unnamed x6, local copies, waits for them, and re-layouts  6.77 us

profile of v2, /device:TPU:11, one launch (start us, length us, event | category | flops | bytes accessed | tf_op | source)
XLA Modules:
  0.0 121.2 jit_solution(4291327747846918694)
XLA Ops:
  0.6 113.8 %shard_map.93 = (bf16[192,1024]{1,0:T(8,128)(2,1)}, bf16[192,1024]{1,0:T(8,128)(2,1)}, bf16[192,1024]{1,0:T(8,128)(2,1)}, bf16[512,2048]{1,0:T(8,128)(2,1)}) custom-call(s32[2]{0:T(128)} %ids_ref.1, bf16[192,1024]{1,0:T(8,128)(2,1)} %bitcast.8, bf16[192,1024]{1,0:T(8,128)(2,1)} %bitcast.9, bf16[192,1024]{1,0:T(8,128)(2,1)} %bitcast.10, ...), custom_call_target="tpu_custom_call" | custom-call | tf_op jit(solution)/shard_map/pallas_call | solution.py:448
  114.5 0.0 copy-start
  114.5 1.9 %copy.14 = bf16[1,192,1024]{2,1,0:T(8,128)(2,1)} copy(bf16[1,192,1024]{2,1,0:T(8,128)(2,1)} %bitcast.13) | data formatting | bytes 786432
  116.4 1.8 %copy.15 = bf16[1,192,1024]{2,1,0:T(8,128)(2,1)} copy(bf16[1,192,1024]{2,1,0:T(8,128)(2,1)} %bitcast.12) | data formatting | bytes 786432
  118.2 1.8 %copy.16 = bf16[1,192,1024]{2,1,0:T(8,128)(2,1)} copy(bf16[1,192,1024]{2,1,0:T(8,128)(2,1)} %bitcast.11) | data formatting | bytes 786432
  119.9 0.0 copy-done
  119.9 1.3 %copy.17 = bf16[512,2048]{1,0:T(8,128)(2,1)} copy(bf16[512,2048]{1,0:T(8,128)(2,1)S(1)} %copy-done) | data formatting | bytes 4194304
Async XLA Ops:
  114.5 5.5 %copy-start = (bf16[512,2048]{1,0:T(8,128)(2,1)S(1)}, bf16[512,2048]{1,0:T(8,128)(2,1)}, u32[]{:S(2)}) copy-start(bf16[512,2048]{1,0:T(8,128)(2,1)} %get-tuple-element.19) | copy-start | bytes 6291460

commit v3 on v2

--- a/solution.py
+++ b/solution.py
@@ -168,6 +168,18 @@
                 pltpu.make_async_copy(src, dst, rsem).start()
         pending.append((copy, same))
 
+    def put_if(cond, src, dst, ssem, rsem, target):
+        copy = pltpu.make_async_remote_copy(
+            src_ref=src, dst_ref=dst, send_sem=ssem, recv_sem=rsem,
+            device_id=target, device_id_type=MESH,
+        )
+
+        @pl.when(cond)
+        def _():
+            copy.start()
+
+        pending.append((copy, jnp.logical_not(cond)))
+
     def keep(src, dst, sem):
         pltpu.make_async_copy(src, dst, sem).start()
 
@@ -291,7 +303,7 @@
         pending.extend((give(o), None) for o in range(1, nz))
         put(atts.at[j, band(z)], attg.at[p], at_s.at[j, 0], at_r.at[p], at(z, h // nd, h % nd), h == p)
 
-    def backward(j):
+    def backward(j, between):
         for o in range(nz):
             arrived(dog.at[j, band(o)], do_r.at[j, o])
         dka[...] = jnp.zeros(dka.shape, F32)
@@ -328,6 +340,7 @@
         keep(dqs.at[j, band(z)], dq_ref.at[:, head_cols(h)], out_r.at[0, h])
         dks[j] = (dka[...] * scale).astype(BF16)
         dvs[j] = dva[...].astype(BF16)
+        between()
         for n, (src, dst) in ((1, (dks, dk_ref)), (2, (dvs, dv_ref))):
             for o in range(1, nz + 1):
                 t = (z + o) % nz
@@ -380,35 +393,54 @@
     def cut_rows(i):
         return pl.ds(pl.multiple_of(i * cut, cut), cut)
 
-    for o in range(1, nz):
-        t = (z + o) % nz
-        put(wpart.at[cut_rows(t)], wrecv.at[z], ws_s.at[o], ws_r.at[z], at(t, f, d))
-
-    backward(0)
-
-    share = wacc[cut_rows(z), :]
-    for o in range(1, nz):
-        t = (z + o) % nz
-        arrived(wrecv.at[t], ws_r.at[t])
-        share = share + wrecv[t].astype(F32)
+    z1 = z + 1 - 2 * (z % 2)
+    z2, z3 = (z + 2) % nz, (z1 + 2) % nz
+    put(wpart.at[cut_rows(z3)], wrecv.at[1], ws_s.at[1], ws_r.at[1], at(z1, f, d))
+    put(wpart.at[cut_rows(z1)], wrecv.at[0], ws_s.at[0], ws_r.at[0], at(z1, f, d))
+
+    def across():
+        arrived(wrecv.at[1], ws_r.at[1])
+        wrecv[3] = (wacc[cut_rows(z2), :] + wrecv[1].astype(F32)).astype(BF16)
+        put(wrecv.at[3], wrecv.at[2], ws_s.at[2], ws_r.at[2], at(z2, f, d))
+
+    backward(0, across)
+
+    arrived(wrecv.at[0], ws_r.at[0])
+    arrived(wrecv.at[2], ws_r.at[2])
+    share = wacc[cut_rows(z), :] + wrecv[0].astype(F32) + wrecv[2].astype(F32)
     wfin[...] = (share * (1.0 / math.sqrt(token_count))).astype(BF16)
 
     def final(dd, zz):
         return dw_ref.at[pl.ds(pl.multiple_of(dd * HD + zz * cut, cut), cut)]
 
-    for o in range(1, nz):
-        put(wfin, final(d, z), wf_s.at[o], wf_r.at[d, z], at((z + o) % nz, f, d))
+    upper, lower = (z + 1) % nz, (z + nz - 1) % nz
+    put_if(z < nz - 1, wfin, final(d, z), wf_s.at[0], wf_r.at[d, z], at(upper, f, d))
+    put_if(z > 0, wfin, final(d, z), wf_s.at[1], wf_r.at[d, z], at(lower, f, d))
     put(wfin, final(d, z), wx_s.at[0], wf_r.at[d, z], at(z, f, dx))
     put(wfin, final(d, z), wc_s.at[0, 0], wf_r.at[d, z], at(z, f, dc))
     keep(wfin, final(d, z), wf_r.at[d, z])
 
-    backward(1)
-
-    for o in range(1, nz):
-        t = (z + o) % nz
-        arrived(final(d, t), wf_r.at[d, t])
-        put(final(d, t), final(d, t), wx_s.at[o], wf_r.at[d, t], at(z, f, dx))
-        put(final(d, t), final(d, t), wc_s.at[0, o], wf_r.at[d, t], at(z, f, dc))
+    def pass_on(far):
+        for side in range(2):
+            t = (z - far + nz) % nz if side == 0 else (z + far) % nz
+            there = z >= far if side == 0 else z < nz - far
+            further = z < nz - 1 if side == 0 else z > 0
+
+            @pl.when(there)
+            def _(t=t):
+                arrived(final(d, t), wf_r.at[d, t])
+
+            piece, n = final(d, t), 2 * far + side
+            put_if(
+                jnp.logical_and(there, further), piece, piece, wf_s.at[n], wf_r.at[d, t],
+                at(upper if side == 0 else lower, f, d),
+            )
+            put_if(there, piece, piece, wx_s.at[n], wf_r.at[d, t], at(z, f, dx))
+            put_if(there, piece, piece, wc_s.at[0, n], wf_r.at[d, t], at(z, f, dc))
+
+    pass_on(1)
+    backward(1, lambda: pass_on(2))
+    pass_on(3)
     for o in range(nz):
         t = (z + o) % nz
         arrived(final(dx, t), wf_r.at[dx, t])
@@ -428,6 +460,22 @@
             @pl.when(jnp.logical_not(same))
             def _(copy=copy):
                 copy.wait_send()
+
+
+def hand_out(*refs):
+    sources, targets, sems = refs[:4], refs[4:8], refs[8]
+    copies = []
+    for n in range(4):
+        part = sources[n].shape[0] // 4
+        for i in range(4):
+            rows = pl.ds(i * part, part)
+            copies.append(
+                pltpu.make_async_copy(sources[n].at[rows], targets[n].at[rows], sems.at[n, i])
+            )
+    for copy in copies:
+        copy.start()
+    for copy in copies:
+        copy.wait()
 
 
 def fused(mesh, query, key, value, out_weight, out_grad, block_ids):
@@ -477,13 +525,21 @@
             dma((local_heads, nz)), dma((plane,)),
             dma((3, local_heads, nz)), dma((3, HEADS)),
             dma((nz,)), dma((nz,)),
-            dma((nz,)), dma((nd, nz)),
-            dma((nz,)), dma((2, nz)),
+            dma((2 * nz,)), dma((nd, nz)),
+            dma((2 * nz,)), dma((2, 2 * nz)),
         ],
         compiler_params=pltpu.CompilerParams(
             collective_id=0, has_side_effects=True, vmem_limit_bytes=60 * 1024 * 1024
         ),
     )(block_ids, query[0], key[0], value[0], out_weight, out_grad[0])
+    results = (dq, dk, dv, dw)
+    dq, dk, dv, dw = pl.pallas_call(
+        hand_out,
+        out_shape=tuple(jax.ShapeDtypeStruct(r.shape, BF16) for r in results),
+        in_specs=[anyspec] * 4,
+        out_specs=(anyspec,) * 4,
+        scratch_shapes=[dma((4, 4))],
+    )(*results)
     return dq[None], dk[None], dv[None], dw
 
 

time: 121 us -> 210 us (1.74)
  the two profiles are of different devices: /device:TPU:11 before, /device:TPU:7 now
where the time goes in v3:
time: 210 us
  Pallas kernels  210 us (100%)
    pallas_call x1, Pallas kernels, fused(): pl.pallas_call(functools.partial(fused_kernel, (nz, nf, nd, blocks)), out...  109 us
    pallas_call x1, Pallas kernels, fused(): pl.pallas_call(hand_out, out_shape=tuple((jax.ShapeDtypeStruct(r.shape, B...  101 us

profile of v3, /device:TPU:7, one launch (start us, length us, event | category | flops | bytes accessed | tf_op | source)
XLA Modules:
  0.0 210.2 jit_solution(9428029501925836336)
XLA Ops:
  0.6 109.0 %shard_map.93 = (bf16[192,1024]{1,0:T(8,128)(2,1)}, bf16[192,1024]{1,0:T(8,128)(2,1)}, bf16[192,1024]{1,0:T(8,128)(2,1)}, bf16[512,2048]{1,0:T(8,128)(2,1)}) custom-call(s32[2]{0:T(128)} %ids_ref.1, bf16[192,1024]{1,0:T(8,128)(2,1)} %bitcast.8, bf16[192,1024]{1,0:T(8,128)(2,1)} %bitcast.9, bf16[192,1024]{1,0:T(8,128)(2,1)} %bitcast.10, ...), custom_call_target="tpu_custom_call" | custom-call | tf_op jit(solution)/shard_map/pallas_call | solution.py:496
  109.6 100.5 %shard_map.94 = (bf16[192,1024]{1,0:T(8,128)(2,1)}, bf16[192,1024]{1,0:T(8,128)(2,1)}, bf16[192,1024]{1,0:T(8,128)(2,1)}, bf16[512,2048]{1,0:T(8,128)(2,1)}) custom-call(bf16[192,1024]{1,0:T(8,128)(2,1)} %get-tuple-element.12.refs_0_, bf16[192,1024]{1,0:T(8,128)(2,1)} %get-tuple-element.13.refs_1_, bf16[192,1024]{1,0:T(8,128)(2,1)} %get-tuple-element.14.refs_2_, ...), custom_call_target="tpu_custom_call" | custom-call | tf_op jit(solution)/shard_map/pallas_call | solution.py:536

commit v4 on v3

--- a/solution.py
+++ b/solution.py
@@ -129,9 +129,9 @@
 def fused_kernel(
     sizes, ids_ref, q_ref, k_ref, v_ref, w_ref, og_ref, dq_ref, dk_ref, dv_ref, dw_ref,
     blocks_ref, idg, posc, posr, qg, kg, vg, ogall, ws, dos, dog, prob, atts, attg, dqs, dks, dvs, dka, dva,
-    wacc, wpart, wrecv, wfin,
+    wacc, wpart, wrecv, wfin, wall,
     id_s, id_r, in_s, in_r, og_s, og_r, w_sem, do_s, do_r, at_s, at_r, out_s, out_r,
-    ws_s, ws_r, wf_s, wf_r, wx_s, wc_s,
+    ws_s, ws_r, wf_s, wf_r, wx_s, wc_s, wo_s,
 ):
     nz, nf, nd, blocks = sizes
     rows = q_ref.shape[0]
@@ -411,7 +411,7 @@
     wfin[...] = (share * (1.0 / math.sqrt(token_count))).astype(BF16)
 
     def final(dd, zz):
-        return dw_ref.at[pl.ds(pl.multiple_of(dd * HD + zz * cut, cut), cut)]
+        return wall.at[pl.ds(pl.multiple_of(dd * HD + zz * cut, cut), cut)]
 
     upper, lower = (z + 1) % nz, (z + nz - 1) % nz
     put_if(z < nz - 1, wfin, final(d, z), wf_s.at[0], wf_r.at[d, z], at(upper, f, d))
@@ -441,18 +441,26 @@
     pass_on(1)
     backward(1, lambda: pass_on(2))
     pass_on(3)
+    def emit(dd):
+        block = pl.ds(pl.multiple_of(dd * HD, HD), HD)
+        return pltpu.make_async_copy(wall.at[block], dw_ref.at[block], wo_s.at[dd])
+
+    arrived(final(d, z), wf_r.at[d, z])
+    emit(d).start()
     for o in range(nz):
         t = (z + o) % nz
         arrived(final(dx, t), wf_r.at[dx, t])
         put(final(dx, t), final(dx, t), wc_s.at[1, o], wf_r.at[dx, t], at(z, f, dc))
-    dxc = other(dx)
-    arrived(final(d, z), wf_r.at[d, z])
-    for dd in (dc, dxc):
+    emit(dx).start()
+    for dd in (dc, other(dx)):
         for o in range(nz):
             arrived(final(dd, o), wf_r.at[dd, o])
+        emit(dd).start()
     for n, dst in enumerate((dq_ref, dk_ref, dv_ref)):
         for h in range(HEADS):
             arrived(dst.at[:, pl.ds(h * HD, HD)], out_r.at[n, h])
+    for dd in range(nd):
+        emit(dd).wait()
     for copy, same in pending:
         if same is None:
             copy.wait_send()
@@ -463,18 +471,24 @@
 
 
 def hand_out(*refs):
-    sources, targets, sems = refs[:4], refs[4:8], refs[8]
-    copies = []
+    sources, targets, stages, sems = refs[:4], refs[4:8], refs[8:12], refs[12]
+    inward, outward = [], []
     for n in range(4):
         part = sources[n].shape[0] // 4
         for i in range(4):
             rows = pl.ds(i * part, part)
-            copies.append(
-                pltpu.make_async_copy(sources[n].at[rows], targets[n].at[rows], sems.at[n, i])
+            inward.append(
+                pltpu.make_async_copy(sources[n].at[rows], stages[n].at[rows], sems.at[0, n, i])
             )
-    for copy in copies:
+            outward.append(
+                pltpu.make_async_copy(stages[n].at[rows], targets[n].at[rows], sems.at[1, n, i])
+            )
+    for copy in inward:
         copy.start()
-    for copy in copies:
+    for first, second in zip(inward, outward):
+        first.wait()
+        second.start()
+    for copy in outward:
         copy.wait()
 
 
@@ -517,6 +531,7 @@
             vm((HD, model), BF16),
             vm((nz, cut, model), BF16),
             vm((cut, model), BF16),
+            vm(out_weight.shape, BF16),
             dma((nz,)), dma((nz,)),
             dma((3, local_heads, nz)), dma((3, local_heads, nz)),
             dma((9,)), dma((plane, 2)),
@@ -527,6 +542,7 @@
             dma((nz,)), dma((nz,)),
             dma((2 * nz,)), dma((nd, nz)),
             dma((2 * nz,)), dma((2, 2 * nz)),
+            dma((nd,)),
         ],
         compiler_params=pltpu.CompilerParams(
             collective_id=0, has_side_effects=True, vmem_limit_bytes=60 * 1024 * 1024
@@ -538,7 +554,7 @@
         out_shape=tuple(jax.ShapeDtypeStruct(r.shape, BF16) for r in results),
         in_specs=[anyspec] * 4,
         out_specs=(anyspec,) * 4,
-        scratch_shapes=[dma((4, 4))],
+        scratch_shapes=[vm(r.shape, BF16) for r in results] + [dma((2, 4, 4))],
     )(*results)
     return dq[None], dk[None], dv[None], dw
 

time: 210 us -> 113 us (0.54)
  Pallas kernels: 210 us -> 112 us
    pallas_call x1, Pallas kernels: 101 us -> 3.49 us  [fused(): pl.pallas_call(hand_out, out_shape=tuple((jax.ShapeDtypeStruct(r.shape, B...]
where the time goes in v4:
time: 113 us
  Pallas kernels  112 us (99%)
    pallas_call x1, Pallas kernels, fused(): pl.pallas_call(functools.partial(fused_kernel, (nz, nf, nd, blocks)), out...  109 us
    pallas_call x1, Pallas kernels, fused(): pl.pallas_call(hand_out, out_shape=tuple((jax.ShapeDtypeStruct(r.shape, B...  3.49 us

profile of v4, /device:TPU:7, one launch (start us, length us, event | category | flops | bytes accessed | tf_op | source)
XLA Modules:
  0.0 112.8 jit_solution(13630726433552881196)
XLA Ops:
  0.6 108.7 %shard_map.93 = (bf16[192,1024]{1,0:T(8,128)(2,1)}, bf16[192,1024]{1,0:T(8,128)(2,1)}, bf16[192,1024]{1,0:T(8,128)(2,1)}, bf16[512,2048]{1,0:T(8,128)(2,1)}) custom-call(s32[2]{0:T(128)} %ids_ref.1, bf16[192,1024]{1,0:T(8,128)(2,1)} %bitcast.8, bf16[192,1024]{1,0:T(8,128)(2,1)} %bitcast.9, bf16[192,1024]{1,0:T(8,128)(2,1)} %bitcast.10, ...), custom_call_target="tpu_custom_call" | custom-call | tf_op jit(solution)/shard_map/pallas_call | solution.py:510
  109.3 3.5 %shard_map.94 = (bf16[192,1024]{1,0:T(8,128)(2,1)}, bf16[192,1024]{1,0:T(8,128)(2,1)}, bf16[192,1024]{1,0:T(8,128)(2,1)}, bf16[512,2048]{1,0:T(8,128)(2,1)}) custom-call(bf16[192,1024]{1,0:T(8,128)(2,1)} %get-tuple-element.12.refs_0_, bf16[192,1024]{1,0:T(8,128)(2,1)} %get-tuple-element.13.refs_1_, bf16[192,1024]{1,0:T(8,128)(2,1)} %get-tuple-element.14.refs_2_, ...), custom_call_target="tpu_custom_call" | custom-call | tf_op jit(solution)/shard_map/pallas_call | solution.py:552
